TPU v7x, 32 devices: a whole 2x2x4 slice. The times are simulated.
32 devices in a mesh: mem: 8 (over y, x, core), tile: 4 (over z).
Axes of the slice: x: 2, y: 2, z: 4, core: 2. Of those that a mesh axis runs over, the one named last changes fastest.
Arguments:
- latents: bfloat16 [16, 16, 8192], P('mem', 'tile'), may hold values from -3 to 3
- in_weight: bfloat16 [2, 576, 256], replicated, may hold values from -0.25 to 0.25
- out_weight: bfloat16 [2, 2304, 64], replicated, may hold values from -0.125 to 0.125
- observe_weight: bfloat16 [576, 8], replicated, may hold values from -0.25 to 0.25
- obs_cells: int32 [16, 32], P('tile'), may hold values from 0 to 127, all different within a row
- obs_values: float32 [16, 256], P('tile'), may hold values from -6 to 6
- obs_precision: float32 [16, 256], P('tile'), may hold values from 0.3 to 3
Outputs:
- analysis: float32 [16, 16, 8192], P('mem', 'tile')
- covariance: float32 [16, 16], replicated
Inputs may be any that keep to these rules, and one draw needn't show every extreme that they name: `obs_cells`: each row lists 32 different columns of the slab.
All inputs are finite; a program needn't handle non-finite values.
Results may differ from a plain program's by a relative error of at most 0.009.
Values may be sent and summed in bfloat16 or wider, within the bound.
A program may use at most 64 MiB of HBM per device.

v0:
```python
import functools

import jax
import jax.numpy as jnp
from jax import lax
from jax.experimental import pallas as pl
from jax.experimental.pallas import tpu as pltpu
from jax.sharding import PartitionSpec as P

EPS = 1e-06
GUIDE_STEP = 0.5
HALO = 4
BF16 = jnp.bfloat16
F32 = jnp.float32
HIGHEST = lax.Precision.HIGHEST


def iota(shape, axis):
    return lax.broadcasted_iota(jnp.int32, shape, axis)


def neighbours(values, pairs, half, swap):
    count = values.shape[0]
    pair = iota(values.shape, 0) % pairs
    lane = iota(values.shape, 1)
    following = jnp.where(pair == pairs - 1, 0.0, pltpu.roll(values, count - 1, 0))
    previous = jnp.where(pair == 0, 0.0, pltpu.roll(values, 1, 0))
    if swap:
        following, previous = previous, following
    return jnp.where(lane < half, following, previous)


def kernel(
    sizes, lat, w_in, w_out, w_obs, cells, values, precision, out, cov_out,
    halo, stage, raw, frame, hid, cur, big_in, big_out, big_obs, patch, gathered, edge, preds, chunks, covs,
    halo_send, halo_recv, edge_send, edge_recv, pred_send, pred_recv,
    bulk_send, fwd_send, bulk_recv, cov_send, cov_recv,
):
    mem_n, tile_n = sizes
    members, rows, flat_count = lat.shape
    half = w_obs.shape[1] // 9
    lanes = 2 * half
    pairs = flat_count // lanes
    hidden = w_in.shape[2]
    obs_cols = cells.shape[1]
    obs_lanes = values.shape[1]
    obs_ch = w_obs.shape[0]
    ens = mem_n * members
    me, tile = lax.axis_index("mem"), lax.axis_index("tile")
    ext = rows + 2 * HALO

    def mem_peer(k):
        return lax.rem(me + k, mem_n)

    def tile_peer(k):
        return lax.rem(tile + k, tile_n)

    barrier = pltpu.get_barrier_semaphore()
    for k in range(1, mem_n):
        pl.semaphore_signal(barrier, inc=1, device_id={"mem": mem_peer(k)}, device_id_type=pl.DeviceIdType.MESH)
    for k in range(1, tile_n):
        pl.semaphore_signal(barrier, inc=1, device_id={"tile": tile_peer(k)}, device_id_type=pl.DeviceIdType.MESH)
    def remote(src, dst, send, recv, axis, index):
        return pltpu.make_async_remote_copy(
            src_ref=src, dst_ref=dst, send_sem=send, recv_sem=recv,
            device_id={axis: index}, device_id_type=pl.DeviceIdType.MESH,
        )

    to_next = remote(
        lat, halo.at[0], halo_send.at[0], halo_recv.at[0], "tile", jnp.minimum(tile + 1, tile_n - 1)
    )
    to_prev = remote(
        lat, halo.at[1], halo_send.at[1], halo_recv.at[1], "tile", jnp.maximum(tile - 1, 0)
    )
    has_next, has_prev = tile < tile_n - 1, tile > 0

    def build_in(layer):
        zero = jnp.zeros((half, hidden), BF16)
        for di in range(3):
            tap = lambda dj: w_in[layer, pl.ds((di * 3 + dj) * half, half), :]
            blocks = ((tap(1), tap(0)), (tap(2), tap(1)), (zero, tap(2)), (tap(0), zero))
            for b, (even, odd) in enumerate(blocks):
                at = pl.ds((di * 4 + b) * half, half)
                big_in[layer, at, pl.ds(0, hidden)] = even
                big_in[layer, at, pl.ds(hidden, hidden)] = odd

    def build_out(layer):
        zero = jnp.zeros((half, hidden), BF16)
        for di in range(3):
            tap = lambda dj: w_out[layer, :, pl.ds((di * 3 + dj) * hidden, hidden)]
            blocks = ((tap(1), tap(2)), (tap(0), tap(1)), (zero, tap(0)), (tap(2), zero))
            for b, (even, odd) in enumerate(blocks):
                at = pl.ds(b * half, half)
                big_out[layer, at, pl.ds(di * 2 * hidden, hidden)] = even
                big_out[layer, at, pl.ds((di * 2 + 1) * hidden, hidden)] = odd

    def build_obs():
        weight = w_obs[...]
        zero = jnp.zeros((obs_ch, half), BF16)
        blocks = []
        for parity in range(2):
            for di in range(3):
                tap = lambda dj: weight[:, (di * 3 + dj) * half : (di * 3 + dj + 1) * half]
                blocks += [[tap(1), tap(2), zero, tap(0)], [tap(0), tap(1), tap(2), zero]][parity]
        spread_ch = iota((obs_lanes, obs_ch), 0) % obs_ch == iota((obs_lanes, obs_ch), 1)
        big_obs[...] = jnp.dot(
            spread_ch.astype(BF16), jnp.concatenate(blocks, axis=1), preferred_element_type=F32
        ).astype(BF16)

    def unfold(slot, source, m):
        for p in range(pairs):
            tile_p = source[m, :, pl.ds(p * lanes, lanes)] if slot is None else source[slot, m, :, pl.ds(p * lanes, lanes)]
            stage[pl.ds(p * rows, rows), :] = tile_p.astype(F32)

    def unfolded(first, count):
        return jnp.concatenate(
            [stage[pl.ds(first + r, pairs, stride=rows), :] for r in range(count)], axis=0
        )

    def take(slot, source, m, first, start, count):
        unfold(slot, source, m)
        wide = unfolded(first, count)
        put(raw, m, start, count, wide.astype(BF16))
        put(frame, m, start, count, norm_frame(wide))

    ones = (iota((2 * lanes, lanes), 0) // half % 2 == iota((2 * lanes, lanes), 1) // half).astype(BF16)

    def norm_frame(x):
        wide = x.astype(F32)
        square = wide * wide
        high = square.astype(BF16)
        low = (square - high.astype(F32)).astype(BF16)
        total = jnp.dot(jnp.concatenate([high, low], axis=1), ones, preferred_element_type=F32)
        normed = wide * lax.rsqrt(total * (1.0 / half) + EPS)
        return with_sides(normed)

    def with_sides(v):
        return jnp.concatenate([v, neighbours(v, pairs, half, False)], axis=1).astype(BF16)

    def flat(ref, m, start, count):
        return ref[m, pl.ds(start, count)].reshape(count * pairs, ref.shape[-1])

    def put(ref, m, start, count, value):
        ref[m, pl.ds(start, count)] = value.reshape(count, pairs, ref.shape[-1])

    def taps(ref, m, start, count):
        return jnp.concatenate([flat(ref, m, start + d - 1, count) for d in range(3)], axis=1)

    def conv_in(layer, m, start, count):
        summed = jnp.dot(taps(frame, m, start, count), big_in[layer], preferred_element_type=F32)
        act = 0.5 * summed * (1.0 + jnp.tanh(0.5 * summed))
        put(hid, m, start, count, act.astype(BF16))

    def conv_out(layer, m, start, count, before):
        summed = lax.dot_general(
            taps(hid, m, start, count), big_out[layer], (((1,), (1,)), ((), ())), preferred_element_type=F32
        )
        summed = summed[:, :lanes] + neighbours(summed[:, lanes:], pairs, half, True)
        return (before.astype(F32) + summed).astype(BF16)

    def blank(ref, low, high):
        def clear(start, count):
            ref[:, pl.ds(start, count)] = jnp.zeros((members, count) + ref.shape[2:], BF16)
        pl.when(tile == 0)(lambda: clear(low, HALO - low))
        pl.when(tile == tile_n - 1)(lambda: clear(HALO + rows, high - HALO - rows))

    build_in(0)
    pl.semaphore_wait(barrier, mem_n - 1 + tile_n - 1)
    pl.when(has_next)(lambda: to_next.start())
    pl.when(has_prev)(lambda: to_prev.start())
    for m in range(members):
        take(None, lat, m, 0, HALO, rows)
    for m in range(members):
        conv_in(0, m, HALO + 1, rows - 2)
    build_out(0)
    build_in(1)
    build_out(1)
    build_obs()
    eye = (iota((obs_cols, obs_cols), 0) == iota((obs_cols, obs_cols), 1)).astype(BF16)
    cells_t = lax.dot_general(
        eye, cells[...].astype(F32).astype(BF16), (((1,), (1,)), ((), ())), preferred_element_type=F32
    ).astype(jnp.int32)

    pl.when(has_prev)(lambda: to_next.wait_recv())
    pl.when(has_next)(lambda: to_prev.wait_recv())

    @pl.when(tile == 0)
    def _():
        halo[0] = jnp.zeros(halo.shape[1:], BF16)

    @pl.when(tile == tile_n - 1)
    def _():
        halo[1] = jnp.zeros(halo.shape[1:], BF16)

    for m in range(members):
        take(0, halo, m, rows - HALO, 0, HALO)
        take(1, halo, m, 0, HALO + rows, HALO)
        conv_in(0, m, 1, HALO)
        conv_in(0, m, HALO + rows - 1, HALO)
    blank(hid, 1, ext - 1)
    for m in range(members):
        put(cur, m, 2, ext - 4, conv_out(0, m, 2, ext - 4, flat(raw, m, 2, ext - 4)))
    blank(cur, 2, ext - 2)
    for m in range(members):
        put(frame, m, 2, ext - 4, norm_frame(flat(cur, m, 2, ext - 4)))
        conv_in(1, m, 3, ext - 6)
    blank(hid, 3, ext - 3)

    step = 2 if mem_n % 2 == 0 else 1
    sibling = me + 1 - 2 * lax.rem(me, 2)
    edge_next, edge_prev, bulk, forwards = [], [], [], []

    def share(m):
        block = gathered.at[me, m]
        for k in range(step, mem_n, step):
            bulk.append(remote(block, block, bulk_send.at[k, m], bulk_recv.at[me, m], "mem", mem_peer(k)))
        if step == 2:
            bulk.append(remote(block, block, bulk_send.at[0, m], bulk_recv.at[me, m], "mem", sibling))
        for copy in bulk[-(mem_n // step if step == 2 else mem_n - 1):]:
            copy.start()

    def arrived(k, m):
        j = mem_peer(k)
        block = gathered.at[j, m]
        remote(block, block, bulk_send.at[0, m], bulk_recv.at[j, m], "mem", j).wait_recv()

    def pass_on(m):
        if step == 2:
            for k in range(2, mem_n, 2):
                arrived(k, m)
                j = mem_peer(k)
                block = gathered.at[j, m]
                copy = remote(block, block, fwd_send.at[k, m], bulk_recv.at[j, m], "mem", sibling)
                copy.start()
                forwards.append(copy)

    early = (members + 1) // 2
    for m in range(members):
        done = conv_out(1, m, HALO, rows, flat(cur, m, HALO, rows))
        gathered[me, m] = done.reshape(rows, pairs, lanes)
        edge_next.append(remote(
            gathered.at[me, m, rows - 1], edge.at[0, m], edge_send.at[0, m], edge_recv.at[0, m],
            "tile", jnp.minimum(tile + 1, tile_n - 1),
        ))
        edge_prev.append(remote(
            gathered.at[me, m, 0], edge.at[1, m], edge_send.at[1, m], edge_recv.at[1, m],
            "tile", jnp.maximum(tile - 1, 0),
        ))
        pl.when(has_next)(lambda: edge_next[m].start())
        pl.when(has_prev)(lambda: edge_prev[m].start())
        if m < early:
            share(m)

    for m in range(members):
        put(frame, m, HALO, rows, with_sides(gathered[me, m].astype(F32).reshape(rows * pairs, lanes)))
    column = 2 * iota((obs_cols, pairs), 1)
    wide = 12 * half

    def observe(r):
        here = cells_t[:, r : r + 1]
        pick = jnp.concatenate([(here == column), (here == column + 1)], axis=0).astype(BF16)
        around = jnp.concatenate([taps(frame, m, HALO + r, 1) for m in range(members)], axis=1)
        got = jnp.dot(pick, around, preferred_element_type=F32).astype(BF16)
        for m in range(members):
            part = got[:, m * wide : (m + 1) * wide]
            at = pl.ds((m * rows + r) * obs_cols, obs_cols)
            patch[at, pl.ds(0, wide)] = part[:obs_cols]
            patch[at, pl.ds(wide, wide)] = part[obs_cols:]

    for r in range(1, rows - 1):
        observe(r)
    for m in range(members):
        pl.when(has_prev)(lambda: edge_next[m].wait_recv())
        pl.when(has_next)(lambda: edge_prev[m].wait_recv())

    @pl.when(tile == 0)
    def _():
        edge[0] = jnp.zeros(edge.shape[1:], BF16)

    @pl.when(tile == tile_n - 1)
    def _():
        edge[1] = jnp.zeros(edge.shape[1:], BF16)

    for m in range(members):
        frame[m, HALO - 1] = with_sides(edge[0, m].astype(F32))
        frame[m, HALO + rows] = with_sides(edge[1, m].astype(F32))
    for r in sorted({0, rows - 1}):
        observe(r)
    spread_pred = lax.dot_general(
        patch[...], big_obs[...], (((1,), (1,)), ((), ())), preferred_element_type=F32
    )
    spread_pred = spread_pred.reshape(members * rows, obs_cols, obs_lanes)
    own = iota(spread_pred.shape, 1) == iota(spread_pred.shape, 2) // obs_ch
    per = members * rows
    mine_at = pl.ds(pl.multiple_of(me * per, per), per)
    preds[mine_at, :] = jnp.sum(jnp.where(own, spread_pred, 0.0), axis=1)

    pred_copies = [
        remote(preds.at[mine_at], preds.at[mine_at], pred_send.at[k], pred_recv.at[me], "mem", mem_peer(k))
        for k in range(1, mem_n)
    ]
    for copy in pred_copies:
        copy.start()
    for m in range(early, members):
        share(m)
    for m in range(early):
        pass_on(m)
    for k in range(1, mem_n):
        j = mem_peer(k)
        block = preds.at[pl.ds(pl.multiple_of(j * per, per), per)]
        remote(block, block, pred_send.at[k], pred_recv.at[j], "mem", j).wait_recv()

    left, right = [], []
    for c in range(0, obs_lanes, 128):
        chunks[c // 128] = preds[:, pl.ds(c, 128)]
    for r in range(rows):
        for c in range(0, obs_lanes, 128):
            at = pl.ds(c, 128)
            here = chunks[c // 128, pl.ds(r, ens, stride=rows), :]
            mean = jnp.sum(here, axis=0, keepdims=True) * (1.0 / ens)
            left.append((here - mean) * precision[pl.ds(r, 1), at])
            right.append(values[pl.ds(r, 1), at] - here)
    part = lax.dot_general(
        jnp.concatenate(left, axis=1), jnp.concatenate(right, axis=1), (((1,), (1,)), ((), ())),
        precision=HIGHEST, preferred_element_type=F32,
    )
    covs[tile] = jnp.concatenate([part, jnp.zeros((ens, covs.shape[2] - ens), F32)], axis=1)
    cov_copies = [
        remote(covs.at[tile], covs.at[tile], cov_send.at[k], cov_recv.at[tile], "tile", tile_peer(k))
        for k in range(1, tile_n)
    ]
    for copy in cov_copies:
        copy.start()

    for m in range(early, members):
        pass_on(m)
    for k in range(1, tile_n):
        j = tile_peer(k)
        remote(covs.at[j], covs.at[j], cov_send.at[k], cov_recv.at[j], "tile", j).wait_recv()
    cov = covs[0]
    for j in range(1, tile_n):
        cov = cov + covs[j]
    cov = cov[:, :ens] * (1.0 / (rows * tile_n * obs_lanes))
    cov_out[...] = cov
    centred = GUIDE_STEP * (cov - jnp.mean(cov, axis=0, keepdims=True))
    factors = []
    for q in range(members):
        mine = iota((ens, ens), 1) == me * members + q
        column_q = jnp.sum(jnp.where(mine, centred, 0.0), axis=1, keepdims=True)
        factors.append(jnp.broadcast_to(column_q, (ens, lanes)))

    for k in range(1, mem_n, step):
        for m in range(members):
            arrived(k, m)
    for r in range(rows):
        acc = [gathered[me, q, r].astype(F32) for q in range(members)]
        for j in range(ens):
            value = gathered[j // members, j % members, r].astype(F32)
            for q in range(members):
                acc[q] = acc[q] + factors[q][j : j + 1] * value
        for q in range(members):
            out[q, r] = acc[q]

    pl.when(has_next)(lambda: to_next.wait_send())
    pl.when(has_prev)(lambda: to_prev.wait_send())
    for m in range(members):
        pl.when(has_next)(lambda: edge_next[m].wait_send())
        pl.when(has_prev)(lambda: edge_prev[m].wait_send())
    for copy in bulk + pred_copies + cov_copies + forwards:
        copy.wait_send()


def per_device(sizes, latents, in_weight, out_weight, observe_weight, obs_cells, obs_values, obs_precision):
    mem_n, tile_n = sizes
    members, rows, flat_count = latents.shape
    half = observe_weight.shape[0] // 9
    lanes = 2 * half
    pairs = flat_count // lanes
    hidden = in_weight.shape[2]
    obs_cols, obs_lanes = obs_cells.shape[1], obs_values.shape[1]
    ens = mem_n * members
    ext = rows + 2 * HALO
    vmem = pl.BlockSpec(memory_space=pltpu.VMEM)
    dma = pltpu.SemaphoreType.DMA
    analysis, covariance = pl.pallas_call(
        functools.partial(kernel, sizes),
        out_shape=(
            jax.ShapeDtypeStruct((members, rows, pairs, lanes), F32),
            jax.ShapeDtypeStruct((ens, ens), F32),
        ),
        in_specs=[vmem] * 7,
        out_specs=(vmem, vmem),
        scratch_shapes=[
            pltpu.VMEM((2, members, rows, flat_count), BF16),
            pltpu.VMEM((pairs * rows, lanes), F32),
            pltpu.VMEM((members, ext, pairs, lanes), BF16),
            pltpu.VMEM((members, ext, pairs, 2 * lanes), BF16),
            pltpu.VMEM((members, ext, pairs, 2 * hidden), BF16),
            pltpu.VMEM((members, ext, pairs, lanes), BF16),
            pltpu.VMEM((2, 12 * half, 2 * hidden), BF16),
            pltpu.VMEM((2, 2 * lanes, 6 * hidden), BF16),
            pltpu.VMEM((obs_lanes, 24 * half), BF16),
            pltpu.VMEM((members * rows * obs_cols, 24 * half), BF16),
            pltpu.VMEM((mem_n, members, rows, pairs, lanes), BF16),
            pltpu.VMEM((2, members, pairs, lanes), BF16),
            pltpu.VMEM((mem_n * members * rows, obs_lanes), F32),
            pltpu.VMEM((obs_lanes // 128, ens * rows, 128), F32),
            pltpu.VMEM((tile_n, ens, 128), F32),
            dma((2,)), dma((2,)), dma((2, members)), dma((2, members)),
            dma((mem_n,)), dma((mem_n,)),
            dma((mem_n, members)), dma((mem_n, members)), dma((mem_n, members)),
            dma((tile_n,)), dma((tile_n,)),
        ],
        compiler_params=pltpu.CompilerParams(
            collective_id=0, has_side_effects=True, vmem_limit_bytes=48 * 1024 * 1024
        ),
    )(
        latents, in_weight, out_weight.transpose(0, 2, 1), observe_weight.T,
        obs_cells, obs_values, obs_precision,
    )
    return analysis.reshape(members, rows, flat_count), covariance


def solution(mesh):
    in_specs = (
        P("mem", "tile", None), P(), P(), P(), P("tile", None), P("tile", None), P("tile", None),
    )
    out_specs = (P("mem", "tile", None), P())
    sizes = (mesh.shape["mem"], mesh.shape["tile"])
    return jax.shard_map(
        functools.partial(per_device, sizes), mesh=mesh, in_specs=in_specs, out_specs=out_specs, check_vma=False
    )
```

profile of v0, /device:TPU:0, one launch (start us, length us, event | category | flops | bytes accessed | tf_op | source)
XLA Modules:
  0.0 34.8 jit_solution(12359715808820576108)
XLA Ops:
  0.6 0.0 copy-start.6
  0.6 0.7 %copy-done.6 = s32[4,32]{1,0:T(4,128)S(1)} copy-done((s32[4,32]{1,0:T(4,128)S(1)}, s32[4,32]{1,0:T(4,128)}, u32[]{:S(2)}) %copy-start.6) | copy-done | bytes 536
  1.3 0.0 copy-start
  1.3 1.1 %copy-done = bf16[2,576,256]{2,1,0:T(8,128)(2,1)S(1)} copy-done((bf16[2,576,256]{2,1,0:T(8,128)(2,1)S(1)}, bf16[2,576,256]{2,1,0:T(8,128)(2,1)}, u32[]{:S(2)}) %copy-start) | copy-done | bytes 589848
  2.4 0.0 copy-start.1
  2.4 1.1 %copy-done.1 = bf16[2,2304,64]{1,2,0:T(8,128)(2,1)S(1)} copy-done((bf16[2,2304,64]{1,2,0:T(8,128)(2,1)S(1)}, bf16[2,2304,64]{1,2,0:T(8,128)(2,1)}, u32[]{:S(2)}) %copy-start.1) | copy-done | bytes 589848
  3.4 0.0 copy-start.2
  3.4 0.9 %copy-done.2 = bf16[2,4,8192]{2,1,0:T(4,128)(2,1)S(1)} copy-done((bf16[2,4,8192]{2,1,0:T(4,128)(2,1)S(1)}, bf16[2,4,8192]{2,1,0:T(4,128)(2,1)}, u32[]{:S(2)}) %copy-start.2) | copy-done | bytes 131096
  4.3 0.0 copy-start.3
  4.4 0.7 %copy-done.3 = bf16[576,8]{0,1:T(8,128)(2,1)S(1)} copy-done((bf16[576,8]{0,1:T(8,128)(2,1)S(1)}, bf16[576,8]{0,1:T(8,128)(2,1)}, u32[]{:S(2)}) %copy-start.3) | copy-done | bytes 9240
  5.1 0.0 copy-start.4
  5.1 0.7 %copy-done.4 = f32[4,256]{1,0:T(4,128)S(1)} copy-done((f32[4,256]{1,0:T(4,128)S(1)}, f32[4,256]{1,0:T(4,128)}, u32[]{:S(2)}) %copy-start.4) | copy-done | bytes 4120
  5.7 0.0 copy-start.5
  5.7 0.7 %copy-done.5 = f32[4,256]{1,0:T(4,128)S(1)} copy-done((f32[4,256]{1,0:T(4,128)S(1)}, f32[4,256]{1,0:T(4,128)}, u32[]{:S(2)}) %copy-start.5) | copy-done | bytes 4120
  6.4 26.9 %shard_map.86 = (f32[2,4,64,128]{3,2,1,0:T(8,128)S(1)}, f32[16,16]{1,0:T(8,128)S(1)}) custom-call(bf16[2,4,8192]{2,1,0:T(4,128)(2,1)S(1)} %copy-done.2, bf16[2,576,256]{2,1,0:T(8,128)(2,1)S(1)} %copy-done, bf16[2,64,2304]{2,1,0:T(8,128)(2,1)S(1)} %bitcast.4, bf16[8,576]{1,0:T(8,128)(2,1)S(1)} %bitcast.5, s32[4,32]{1,0:T(4,128)S(1)} %copy-done.6, ...), custom_call_target="tpu_custom_call" | custom-call | tf_op jit(solution)/shard_map/pallas_call | solution.py:385
  33.4 0.8 %reshape.7 = f32[2,4,8192]{2,1,0:T(4,128)} reshape(f32[2,4,64,128]{3,2,1,0:T(8,128)S(1)} %get-tuple-element.4) | data formatting | bytes 524288 | tf_op jit(solution)/shard_map/reshape | solution.py:421
  34.2 0.6 %copy.10 = f32[16,16]{1,0:T(8,128)} copy(f32[16,16]{1,0:T(8,128)S(1)} %get-tuple-element.9) | data formatting | bytes 2048
Async XLA Ops:
  0.6 0.7 %copy-start.6 = (s32[4,32]{1,0:T(4,128)S(1)}, s32[4,32]{1,0:T(4,128)}, u32[]{:S(2)}) copy-start(s32[4,32]{1,0:T(4,128)} %cells.1) | copy-start | bytes 1540
  1.3 1.1 %copy-start = (bf16[2,576,256]{2,1,0:T(8,128)(2,1)S(1)}, bf16[2,576,256]{2,1,0:T(8,128)(2,1)}, u32[]{:S(2)}) copy-start(bf16[2,576,256]{2,1,0:T(8,128)(2,1)} %w_in.1) | copy-start | bytes 1769476
  2.4 1.1 %copy-start.1 = (bf16[2,2304,64]{1,2,0:T(8,128)(2,1)S(1)}, bf16[2,2304,64]{1,2,0:T(8,128)(2,1)}, u32[]{:S(2)}) copy-start(bf16[2,2304,64]{1,2,0:T(8,128)(2,1)} %param.9) | copy-start | bytes 1769476
  3.4 0.9 %copy-start.2 = (bf16[2,4,8192]{2,1,0:T(4,128)(2,1)S(1)}, bf16[2,4,8192]{2,1,0:T(4,128)(2,1)}, u32[]{:S(2)}) copy-start(bf16[2,4,8192]{2,1,0:T(4,128)(2,1)} %lat.1) | copy-start | bytes 393220
  4.3 0.7 %copy-start.3 = (bf16[576,8]{0,1:T(8,128)(2,1)S(1)}, bf16[576,8]{0,1:T(8,128)(2,1)}, u32[]{:S(2)}) copy-start(bf16[576,8]{0,1:T(8,128)(2,1)} %param.10) | copy-start | bytes 27652
  5.1 0.7 %copy-start.4 = (f32[4,256]{1,0:T(4,128)S(1)}, f32[4,256]{1,0:T(4,128)}, u32[]{:S(2)}) copy-start(f32[4,256]{1,0:T(4,128)} %values.1) | copy-start | bytes 12292
  5.7 0.7 %copy-start.5 = (f32[4,256]{1,0:T(4,128)S(1)}, f32[4,256]{1,0:T(4,128)}, u32[]{:S(2)}) copy-start(f32[4,256]{1,0:T(4,128)} %precision.1) | copy-start | bytes 12292
where the time goes:
time: 35.1 us; the launch traced here: 34.8 us
  Pallas kernels  26.9 us (77%)
  local copies, waits for them, and re-layouts  7.19 us (20%)
  between operations  0.66 us (2%)
    pallas_call x1, Pallas kernels, per_device(): pl.pallas_call(functools.partial(kernel, sizes), out_shape=(jax.ShapeDtyp...  26.9 us
    unnamed x15, local copies, waits for them, and re-layouts  6.38 us
    reshape x1, local copies, waits for them, and re-layouts, per_device(): return (analysis.reshape(members, rows, flat_count), covariance)  0.81 us

commit v1 on v0

--- a/solution.py
+++ b/solution.py
@@ -20,23 +20,31 @@
 
 
 def neighbours(values, pairs, half, swap):
-    count = values.shape[0]
-    pair = iota(values.shape, 0) % pairs
-    lane = iota(values.shape, 1)
-    following = jnp.where(pair == pairs - 1, 0.0, pltpu.roll(values, count - 1, 0))
-    previous = jnp.where(pair == 0, 0.0, pltpu.roll(values, 1, 0))
+    count, lanes = values.shape
+    pair = iota((1, pairs, lanes), 1)
+    low = iota((1, pairs, lanes), 2) < half
+    following = pltpu.roll(values, count - 1, 0).reshape(count // pairs, pairs, lanes)
+    previous = pltpu.roll(values, 1, 0).reshape(count // pairs, pairs, lanes)
     if swap:
-        following, previous = previous, following
-    return jnp.where(lane < half, following, previous)
+        outside = (low & (pair == 0)) | (~low & (pair == pairs - 1))
+        picked = jnp.where(low, previous, following)
+    else:
+        outside = (low & (pair == pairs - 1)) | (~low & (pair == 0))
+        picked = jnp.where(low, following, previous)
+    return jnp.where(outside, 0.0, picked).reshape(count, lanes)
 
 
 def kernel(
-    sizes, lat, w_in, w_out, w_obs, cells, values, precision, out, cov_out,
+    sizes, *refs
+):
+    mem_n, tile_n = sizes
+    operands, (out, cov_out), local, load_sem, rest = refs[:7], refs[7:9], refs[9:16], refs[16], refs[17:]
+    lat, w_in, w_out, w_obs, cells, values, precision = local
+    (
     halo, stage, raw, frame, hid, cur, big_in, big_out, big_obs, patch, gathered, edge, preds, chunks, covs,
     halo_send, halo_recv, edge_send, edge_recv, pred_send, pred_recv,
     bulk_send, fwd_send, bulk_recv, cov_send, cov_recv,
-):
-    mem_n, tile_n = sizes
+    ) = rest
     members, rows, flat_count = lat.shape
     half = w_obs.shape[1] // 9
     lanes = 2 * half
@@ -55,6 +63,12 @@
     def tile_peer(k):
         return lax.rem(tile + k, tile_n)
 
+    loads = [
+        pltpu.make_async_copy(source, dest, load_sem.at[i])
+        for i, (source, dest) in enumerate(zip(operands, local))
+    ]
+    for load in loads:
+        load.start()
     barrier = pltpu.get_barrier_semaphore()
     for k in range(1, mem_n):
         pl.semaphore_signal(barrier, inc=1, device_id={"mem": mem_peer(k)}, device_id_type=pl.DeviceIdType.MESH)
@@ -67,17 +81,17 @@
         )
 
     to_next = remote(
-        lat, halo.at[0], halo_send.at[0], halo_recv.at[0], "tile", jnp.minimum(tile + 1, tile_n - 1)
+        operands[0], halo.at[0], halo_send.at[0], halo_recv.at[0], "tile", jnp.minimum(tile + 1, tile_n - 1)
     )
     to_prev = remote(
-        lat, halo.at[1], halo_send.at[1], halo_recv.at[1], "tile", jnp.maximum(tile - 1, 0)
+        operands[0], halo.at[1], halo_send.at[1], halo_recv.at[1], "tile", jnp.maximum(tile - 1, 0)
     )
     has_next, has_prev = tile < tile_n - 1, tile > 0
 
     def build_in(layer):
         zero = jnp.zeros((half, hidden), BF16)
         for di in range(3):
-            tap = lambda dj: w_in[layer, pl.ds((di * 3 + dj) * half, half), :]
+            tap = lambda dj: w_in[layer, pl.ds((di * 3 + dj) * half, half), :] * BF16(0.5)
             blocks = ((tap(1), tap(0)), (tap(2), tap(1)), (zero, tap(2)), (tap(0), zero))
             for b, (even, odd) in enumerate(blocks):
                 at = pl.ds((di * 4 + b) * half, half)
@@ -102,7 +116,8 @@
             for di in range(3):
                 tap = lambda dj: weight[:, (di * 3 + dj) * half : (di * 3 + dj + 1) * half]
                 blocks += [[tap(1), tap(2), zero, tap(0)], [tap(0), tap(1), tap(2), zero]][parity]
-        spread_ch = iota((obs_lanes, obs_ch), 0) % obs_ch == iota((obs_lanes, obs_ch), 1)
+        same_ch = (iota((obs_ch, obs_ch), 0) == iota((obs_ch, obs_ch), 1)).astype(F32)
+        spread_ch = jnp.concatenate([same_ch] * obs_cols, axis=0)
         big_obs[...] = jnp.dot(
             spread_ch.astype(BF16), jnp.concatenate(blocks, axis=1), preferred_element_type=F32
         ).astype(BF16)
@@ -123,7 +138,8 @@
         put(raw, m, start, count, wide.astype(BF16))
         put(frame, m, start, count, norm_frame(wide))
 
-    ones = (iota((2 * lanes, lanes), 0) // half % 2 == iota((2 * lanes, lanes), 1) // half).astype(BF16)
+    block = ((iota((lanes, lanes), 0) < half) == (iota((lanes, lanes), 1) < half)).astype(BF16)
+    ones = jnp.concatenate([block, block], axis=0)
 
     def norm_frame(x):
         wide = x.astype(F32)
@@ -148,7 +164,7 @@
 
     def conv_in(layer, m, start, count):
         summed = jnp.dot(taps(frame, m, start, count), big_in[layer], preferred_element_type=F32)
-        act = 0.5 * summed * (1.0 + jnp.tanh(0.5 * summed))
+        act = summed + summed * jnp.tanh(summed)
         put(hid, m, start, count, act.astype(BF16))
 
     def conv_out(layer, m, start, count, before):
@@ -164,14 +180,22 @@
         pl.when(tile == 0)(lambda: clear(low, HALO - low))
         pl.when(tile == tile_n - 1)(lambda: clear(HALO + rows, high - HALO - rows))
 
-    build_in(0)
+    def each_member(body):
+        def step_m(m, carry):
+            body(m)
+            return carry
+        lax.fori_loop(0, members, step_m, 0)
+
     pl.semaphore_wait(barrier, mem_n - 1 + tile_n - 1)
     pl.when(has_next)(lambda: to_next.start())
     pl.when(has_prev)(lambda: to_prev.start())
-    for m in range(members):
-        take(None, lat, m, 0, HALO, rows)
-    for m in range(members):
-        conv_in(0, m, HALO + 1, rows - 2)
+    loads[0].wait()
+    each_member(lambda m: take(None, lat, m, 0, HALO, rows))
+    loads[1].wait()
+    build_in(0)
+    each_member(lambda m: conv_in(0, m, HALO + 1, rows - 2))
+    for load in loads[2:]:
+        load.wait()
     build_out(0)
     build_in(1)
     build_out(1)
@@ -192,18 +216,24 @@
     def _():
         halo[1] = jnp.zeros(halo.shape[1:], BF16)
 
-    for m in range(members):
+    def outer_rows(m):
         take(0, halo, m, rows - HALO, 0, HALO)
         take(1, halo, m, 0, HALO + rows, HALO)
         conv_in(0, m, 1, HALO)
         conv_in(0, m, HALO + rows - 1, HALO)
-    blank(hid, 1, ext - 1)
-    for m in range(members):
+
+    def first_out(m):
         put(cur, m, 2, ext - 4, conv_out(0, m, 2, ext - 4, flat(raw, m, 2, ext - 4)))
-    blank(cur, 2, ext - 2)
-    for m in range(members):
+
+    def second_in(m):
         put(frame, m, 2, ext - 4, norm_frame(flat(cur, m, 2, ext - 4)))
         conv_in(1, m, 3, ext - 6)
+
+    each_member(outer_rows)
+    blank(hid, 1, ext - 1)
+    each_member(first_out)
+    blank(cur, 2, ext - 2)
+    each_member(second_in)
     blank(hid, 3, ext - 3)
 
     step = 2 if mem_n % 2 == 0 else 1
@@ -290,7 +320,9 @@
         patch[...], big_obs[...], (((1,), (1,)), ((), ())), preferred_element_type=F32
     )
     spread_pred = spread_pred.reshape(members * rows, obs_cols, obs_lanes)
-    own = iota(spread_pred.shape, 1) == iota(spread_pred.shape, 2) // obs_ch
+    first_lane = iota((1, obs_cols, obs_lanes), 1) * obs_ch
+    lane = iota((1, obs_cols, obs_lanes), 2)
+    own = (lane >= first_lane) & (lane < first_lane + obs_ch)
     per = members * rows
     mine_at = pl.ds(pl.multiple_of(me * per, per), per)
     preds[mine_at, :] = jnp.sum(jnp.where(own, spread_pred, 0.0), axis=1)
@@ -352,7 +384,7 @@
     for k in range(1, mem_n, step):
         for m in range(members):
             arrived(k, m)
-    for r in range(rows):
+    def update_row(r, carry):
         acc = [gathered[me, q, r].astype(F32) for q in range(members)]
         for j in range(ens):
             value = gathered[j // members, j % members, r].astype(F32)
@@ -360,6 +392,9 @@
                 acc[q] = acc[q] + factors[q][j : j + 1] * value
         for q in range(members):
             out[q, r] = acc[q]
+        return carry
+
+    lax.fori_loop(0, rows, update_row, 0)
 
     pl.when(has_next)(lambda: to_next.wait_send())
     pl.when(has_prev)(lambda: to_prev.wait_send())
@@ -380,6 +415,9 @@
     obs_cols, obs_lanes = obs_cells.shape[1], obs_values.shape[1]
     ens = mem_n * members
     ext = rows + 2 * HALO
+    operands = (
+        latents, in_weight, out_weight.transpose(0, 2, 1), observe_weight.T, obs_cells, obs_values, obs_precision
+    )
     vmem = pl.BlockSpec(memory_space=pltpu.VMEM)
     dma = pltpu.SemaphoreType.DMA
     analysis, covariance = pl.pallas_call(
@@ -388,9 +426,10 @@
             jax.ShapeDtypeStruct((members, rows, pairs, lanes), F32),
             jax.ShapeDtypeStruct((ens, ens), F32),
         ),
-        in_specs=[vmem] * 7,
+        in_specs=[pl.BlockSpec(memory_space=pltpu.HBM)] * 7,
         out_specs=(vmem, vmem),
-        scratch_shapes=[
+        scratch_shapes=[pltpu.VMEM(x.shape, x.dtype) for x in operands] + [
+            dma((7,)),
             pltpu.VMEM((2, members, rows, flat_count), BF16),
             pltpu.VMEM((pairs * rows, lanes), F32),
             pltpu.VMEM((members, ext, pairs, lanes), BF16),
@@ -412,12 +451,9 @@
             dma((tile_n,)), dma((tile_n,)),
         ],
         compiler_params=pltpu.CompilerParams(
-            collective_id=0, has_side_effects=True, vmem_limit_bytes=48 * 1024 * 1024
+            collective_id=0, has_side_effects=True, vmem_limit_bytes=32 * 1024 * 1024
         ),
-    )(
-        latents, in_weight, out_weight.transpose(0, 2, 1), observe_weight.T,
-        obs_cells, obs_values, obs_precision,
-    )
+    )(*operands)
     return analysis.reshape(members, rows, flat_count), covariance
 
 

time: 35.1 us -> 35.7 us (1.017)
  Pallas kernels: 26.9 us -> 27.5 us
    pallas_call x1, Pallas kernels: 26.9 us -> 27.5 us  [per_device(): pl.pallas_call(functools.partial(kernel, sizes), out_shape=(jax.ShapeDtyp...]
where the time goes in v1:
time: 35.7 us; the launch traced here: 35.4 us
  Pallas kernels  27.5 us (77%)
  local copies, waits for them, and re-layouts  7.19 us (20%)
  between operations  0.66 us (2%)
    pallas_call x1, Pallas kernels, per_device(): pl.pallas_call(functools.partial(kernel, sizes), out_shape=(jax.ShapeDtyp...  27.5 us
    unnamed x15, local copies, waits for them, and re-layouts  6.38 us
    reshape x1, local copies, waits for them, and re-layouts, per_device(): return (analysis.reshape(members, rows, flat_count), covariance)  0.81 us

profile of v1, /device:TPU:0, one launch (start us, length us, event | category | flops | bytes accessed | tf_op | source)
XLA Modules:
  0.0 35.4 jit_solution(15986614229456067640)
XLA Ops:
  0.6 0.0 copy-start.6
  0.6 0.7 %copy-done.6 = s32[4,32]{1,0:T(4,128)S(1)} copy-done((s32[4,32]{1,0:T(4,128)S(1)}, s32[4,32]{1,0:T(4,128)}, u32[]{:S(2)}) %copy-start.6) | copy-done | bytes 536
  1.3 0.0 copy-start
  1.3 1.1 %copy-done = bf16[2,576,256]{2,1,0:T(8,128)(2,1)S(1)} copy-done((bf16[2,576,256]{2,1,0:T(8,128)(2,1)S(1)}, bf16[2,576,256]{2,1,0:T(8,128)(2,1)}, u32[]{:S(2)}) %copy-start) | copy-done | bytes 589848
  2.4 0.0 copy-start.1
  2.4 1.1 %copy-done.1 = bf16[2,2304,64]{1,2,0:T(8,128)(2,1)S(1)} copy-done((bf16[2,2304,64]{1,2,0:T(8,128)(2,1)S(1)}, bf16[2,2304,64]{1,2,0:T(8,128)(2,1)}, u32[]{:S(2)}) %copy-start.1) | copy-done | bytes 589848
  3.4 0.0 copy-start.2
  3.4 0.9 %copy-done.2 = bf16[2,4,8192]{2,1,0:T(4,128)(2,1)S(1)} copy-done((bf16[2,4,8192]{2,1,0:T(4,128)(2,1)S(1)}, bf16[2,4,8192]{2,1,0:T(4,128)(2,1)}, u32[]{:S(2)}) %copy-start.2) | copy-done | bytes 131096
  4.3 0.0 copy-start.3
  4.4 0.7 %copy-done.3 = bf16[576,8]{0,1:T(8,128)(2,1)S(1)} copy-done((bf16[576,8]{0,1:T(8,128)(2,1)S(1)}, bf16[576,8]{0,1:T(8,128)(2,1)}, u32[]{:S(2)}) %copy-start.3) | copy-done | bytes 9240
  5.1 0.0 copy-start.4
  5.1 0.7 %copy-done.4 = f32[4,256]{1,0:T(4,128)S(1)} copy-done((f32[4,256]{1,0:T(4,128)S(1)}, f32[4,256]{1,0:T(4,128)}, u32[]{:S(2)}) %copy-start.4) | copy-done | bytes 4120
  5.7 0.0 copy-start.5
  5.7 0.7 %copy-done.5 = f32[4,256]{1,0:T(4,128)S(1)} copy-done((f32[4,256]{1,0:T(4,128)S(1)}, f32[4,256]{1,0:T(4,128)}, u32[]{:S(2)}) %copy-start.5) | copy-done | bytes 4120
  6.4 27.5 %shard_map.86 = (f32[2,4,64,128]{3,2,1,0:T(8,128)S(1)}, f32[16,16]{1,0:T(8,128)S(1)}) custom-call(bf16[2,4,8192]{2,1,0:T(4,128)(2,1)S(1)} %copy-done.2, bf16[2,576,256]{2,1,0:T(8,128)(2,1)S(1)} %copy-done, bf16[2,64,2304]{2,1,0:T(8,128)(2,1)S(1)} %bitcast.4, bf16[8,576]{1,0:T(8,128)(2,1)S(1)} %bitcast.5, s32[4,32]{1,0:T(4,128)S(1)} %copy-done.6, ...), custom_call_target="tpu_custom_call" | custom-call | tf_op jit(solution)/shard_map/pallas_call | solution.py:423
  34.0 0.8 %reshape.7 = f32[2,4,8192]{2,1,0:T(4,128)} reshape(f32[2,4,64,128]{3,2,1,0:T(8,128)S(1)} %get-tuple-element.4) | data formatting | bytes 524288 | tf_op jit(solution)/shard_map/reshape | solution.py:457
  34.8 0.6 %copy.10 = f32[16,16]{1,0:T(8,128)} copy(f32[16,16]{1,0:T(8,128)S(1)} %get-tuple-element.9) | data formatting | bytes 2048
Async XLA Ops:
  0.6 0.7 %copy-start.6 = (s32[4,32]{1,0:T(4,128)S(1)}, s32[4,32]{1,0:T(4,128)}, u32[]{:S(2)}) copy-start(s32[4,32]{1,0:T(4,128)} %refs_4_.1) | copy-start | bytes 1540
  1.3 1.1 %copy-start = (bf16[2,576,256]{2,1,0:T(8,128)(2,1)S(1)}, bf16[2,576,256]{2,1,0:T(8,128)(2,1)}, u32[]{:S(2)}) copy-start(bf16[2,576,256]{2,1,0:T(8,128)(2,1)} %refs_1_.1) | copy-start | bytes 1769476
  2.4 1.1 %copy-start.1 = (bf16[2,2304,64]{1,2,0:T(8,128)(2,1)S(1)}, bf16[2,2304,64]{1,2,0:T(8,128)(2,1)}, u32[]{:S(2)}) copy-start(bf16[2,2304,64]{1,2,0:T(8,128)(2,1)} %param.9) | copy-start | bytes 1769476
  3.4 0.9 %copy-start.2 = (bf16[2,4,8192]{2,1,0:T(4,128)(2,1)S(1)}, bf16[2,4,8192]{2,1,0:T(4,128)(2,1)}, u32[]{:S(2)}) copy-start(bf16[2,4,8192]{2,1,0:T(4,128)(2,1)} %refs_0_.1) | copy-start | bytes 393220
  4.3 0.7 %copy-start.3 = (bf16[576,8]{0,1:T(8,128)(2,1)S(1)}, bf16[576,8]{0,1:T(8,128)(2,1)}, u32[]{:S(2)}) copy-start(bf16[576,8]{0,1:T(8,128)(2,1)} %param.10) | copy-start | bytes 27652
  5.1 0.7 %copy-start.4 = (f32[4,256]{1,0:T(4,128)S(1)}, f32[4,256]{1,0:T(4,128)}, u32[]{:S(2)}) copy-start(f32[4,256]{1,0:T(4,128)} %refs_5_.1) | copy-start | bytes 12292
  5.7 0.7 %copy-start.5 = (f32[4,256]{1,0:T(4,128)S(1)}, f32[4,256]{1,0:T(4,128)}, u32[]{:S(2)}) copy-start(f32[4,256]{1,0:T(4,128)} %refs_6_.1) | copy-start | bytes 12292

commit v2 on v1

--- a/solution.py
+++ b/solution.py
@@ -167,12 +167,15 @@
         act = summed + summed * jnp.tanh(summed)
         put(hid, m, start, count, act.astype(BF16))
 
-    def conv_out(layer, m, start, count, before):
+    def conv_sum(layer, lhs, before):
         summed = lax.dot_general(
-            taps(hid, m, start, count), big_out[layer], (((1,), (1,)), ((), ())), preferred_element_type=F32
+            lhs, big_out[layer], (((1,), (1,)), ((), ())), preferred_element_type=F32
         )
         summed = summed[:, :lanes] + neighbours(summed[:, lanes:], pairs, half, True)
         return (before.astype(F32) + summed).astype(BF16)
+
+    def conv_out(layer, m, start, count, before):
+        return conv_sum(layer, taps(hid, m, start, count), before)
 
     def blank(ref, low, high):
         def clear(start, count):
@@ -265,9 +268,21 @@
                 forwards.append(copy)
 
     early = (members + 1) // 2
+
+    def finish(picked):
+        lhs = jnp.concatenate([taps(hid, m, HALO + r, count) for m, r, count in picked], axis=0)
+        before = jnp.concatenate([flat(cur, m, HALO + r, count) for m, r, count in picked], axis=0)
+        done = conv_sum(1, lhs, before)
+        sides = with_sides(done.astype(F32))
+        at = 0
+        for m, r, count in picked:
+            end = at + count * pairs
+            gathered[me, m, pl.ds(r, count)] = done[at:end].reshape(count, pairs, lanes)
+            put(frame, m, HALO + r, count, sides[at:end])
+            at = end
+
+    finish([(m, r, 1) for m in range(members) for r in sorted({0, rows - 1})])
     for m in range(members):
-        done = conv_out(1, m, HALO, rows, flat(cur, m, HALO, rows))
-        gathered[me, m] = done.reshape(rows, pairs, lanes)
         edge_next.append(remote(
             gathered.at[me, m, rows - 1], edge.at[0, m], edge_send.at[0, m], edge_recv.at[0, m],
             "tile", jnp.minimum(tile + 1, tile_n - 1),
@@ -278,11 +293,10 @@
         ))
         pl.when(has_next)(lambda: edge_next[m].start())
         pl.when(has_prev)(lambda: edge_prev[m].start())
-        if m < early:
-            share(m)
-
-    for m in range(members):
-        put(frame, m, HALO, rows, with_sides(gathered[me, m].astype(F32).reshape(rows * pairs, lanes)))
+    finish([(m, 1, rows - 2) for m in range(members)])
+    for m in range(early):
+        share(m)
+
     column = 2 * iota((obs_cols, pairs), 1)
     wide = 12 * half
 
@@ -451,7 +465,7 @@
             dma((tile_n,)), dma((tile_n,)),
         ],
         compiler_params=pltpu.CompilerParams(
-            collective_id=0, has_side_effects=True, vmem_limit_bytes=32 * 1024 * 1024
+            collective_id=0, has_side_effects=True, vmem_limit_bytes=56 * 1024 * 1024
         ),
     )(*operands)
     return analysis.reshape(members, rows, flat_count), covariance

time: 35.7 us -> 30.9 us (0.87)
  local copies, waits for them, and re-layouts: 7.19 us -> 2.37 us
    unnamed x15 -> x3, local copies, waits for them, and re-layouts: 6.38 us -> 0.6 us
    reshape x1, local copies, waits for them, and re-layouts: 0.81 us -> 1.76 us  [per_device(): return (analysis.reshape(members, rows, flat_count), covariance)]
where the time goes in v2:
time: 30.9 us; the launch traced here: 30.8 us
  Pallas kernels  27.8 us (90%)
  local copies, waits for them, and re-layouts  2.37 us (8%)
  between operations  0.65 us (2%)
    pallas_call x1, Pallas kernels, per_device(): pl.pallas_call(functools.partial(kernel, sizes), out_shape=(jax.ShapeDtyp...  27.8 us
    reshape x1, local copies, waits for them, and re-layouts, per_device(): return (analysis.reshape(members, rows, flat_count), covariance)  1.76 us

profile of v2, /device:TPU:0, one launch (start us, length us, event | category | flops | bytes accessed | tf_op | source)
XLA Modules:
  0.0 30.8 jit_solution(1162290564572090141)
XLA Ops:
  0.6 27.8 %shard_map.86 = (f32[2,4,64,128]{3,2,1,0:T(8,128)}, f32[16,16]{1,0:T(8,128)}) custom-call(bf16[2,4,8192]{2,1,0:T(4,128)(2,1)} %refs_0_.1, bf16[2,576,256]{2,1,0:T(8,128)(2,1)} %refs_1_.1, bf16[2,64,2304]{2,1,0:T(8,128)(2,1)} %bitcast.4, bf16[8,576]{1,0:T(8,128)(2,1)} %bitcast.5, s32[4,32]{1,0:T(4,128)} %refs_4_.1, f32[4,256]{1,0:T(4,128)} %refs_5_.1, ...), custom_call_target="tpu_custom_call" | custom-call | tf_op jit(solution)/shard_map/pallas_call | solution.py:437
  28.4 0.0 copy-start
  28.4 1.8 %reshape.7 = f32[2,4,8192]{2,1,0:T(4,128)} reshape(f32[2,4,64,128]{3,2,1,0:T(8,128)} %get-tuple-element.4) | data formatting | bytes 524288 | tf_op jit(solution)/shard_map/reshape | solution.py:471
  30.2 0.0 copy-done
  30.2 0.6 %copy.10 = f32[16,16]{1,0:T(8,128)} copy(f32[16,16]{1,0:T(8,128)S(1)} %copy-done) | data formatting | bytes 2048
Async XLA Ops:
  28.4 1.8 %copy-start = (f32[16,16]{1,0:T(8,128)S(1)}, f32[16,16]{1,0:T(8,128)}, u32[]{:S(2)}) copy-start(f32[16,16]{1,0:T(8,128)} %get-tuple-element.9) | copy-start | bytes 3076

commit v3 on v2

--- a/solution.py
+++ b/solution.py
@@ -80,12 +80,14 @@
             device_id={axis: index}, device_id_type=pl.DeviceIdType.MESH,
         )
 
-    to_next = remote(
-        operands[0], halo.at[0], halo_send.at[0], halo_recv.at[0], "tile", jnp.minimum(tile + 1, tile_n - 1)
-    )
-    to_prev = remote(
-        operands[0], halo.at[1], halo_send.at[1], halo_recv.at[1], "tile", jnp.maximum(tile - 1, 0)
-    )
+    to_next = [remote(
+        operands[0].at[m], halo.at[0, m], halo_send.at[0, m], halo_recv.at[0, m],
+        "tile", jnp.minimum(tile + 1, tile_n - 1),
+    ) for m in range(members)]
+    to_prev = [remote(
+        operands[0].at[m], halo.at[1, m], halo_send.at[1, m], halo_recv.at[1, m],
+        "tile", jnp.maximum(tile - 1, 0),
+    ) for m in range(members)]
     has_next, has_prev = tile < tile_n - 1, tile > 0
 
     def build_in(layer):
@@ -125,16 +127,16 @@
     def unfold(slot, source, m):
         for p in range(pairs):
             tile_p = source[m, :, pl.ds(p * lanes, lanes)] if slot is None else source[slot, m, :, pl.ds(p * lanes, lanes)]
-            stage[pl.ds(p * rows, rows), :] = tile_p.astype(F32)
-
-    def unfolded(first, count):
+            stage[m, pl.ds(p * rows, rows), :] = tile_p.astype(F32)
+
+    def unfolded(m, first, count):
         return jnp.concatenate(
-            [stage[pl.ds(first + r, pairs, stride=rows), :] for r in range(count)], axis=0
+            [stage[m, pl.ds(first + r, pairs, stride=rows), :] for r in range(count)], axis=0
         )
 
     def take(slot, source, m, first, start, count):
         unfold(slot, source, m)
-        wide = unfolded(first, count)
+        wide = unfolded(m, first, count)
         put(raw, m, start, count, wide.astype(BF16))
         put(frame, m, start, count, norm_frame(wide))
 
@@ -184,14 +186,13 @@
         pl.when(tile == tile_n - 1)(lambda: clear(HALO + rows, high - HALO - rows))
 
     def each_member(body):
-        def step_m(m, carry):
+        for m in range(members):
             body(m)
-            return carry
-        lax.fori_loop(0, members, step_m, 0)
 
     pl.semaphore_wait(barrier, mem_n - 1 + tile_n - 1)
-    pl.when(has_next)(lambda: to_next.start())
-    pl.when(has_prev)(lambda: to_prev.start())
+    for m in range(members):
+        pl.when(has_next)(lambda: to_next[m].start())
+        pl.when(has_prev)(lambda: to_prev[m].start())
     loads[0].wait()
     each_member(lambda m: take(None, lat, m, 0, HALO, rows))
     loads[1].wait()
@@ -208,9 +209,6 @@
         eye, cells[...].astype(F32).astype(BF16), (((1,), (1,)), ((), ())), preferred_element_type=F32
     ).astype(jnp.int32)
 
-    pl.when(has_prev)(lambda: to_next.wait_recv())
-    pl.when(has_next)(lambda: to_prev.wait_recv())
-
     @pl.when(tile == 0)
     def _():
         halo[0] = jnp.zeros(halo.shape[1:], BF16)
@@ -220,6 +218,8 @@
         halo[1] = jnp.zeros(halo.shape[1:], BF16)
 
     def outer_rows(m):
+        pl.when(has_prev)(lambda: to_next[m].wait_recv())
+        pl.when(has_next)(lambda: to_prev[m].wait_recv())
         take(0, halo, m, rows - HALO, 0, HALO)
         take(1, halo, m, 0, HALO + rows, HALO)
         conv_in(0, m, 1, HALO)
@@ -300,47 +300,51 @@
     column = 2 * iota((obs_cols, pairs), 1)
     wide = 12 * half
 
-    def observe(r):
-        here = cells_t[:, r : r + 1]
-        pick = jnp.concatenate([(here == column), (here == column + 1)], axis=0).astype(BF16)
-        around = jnp.concatenate([taps(frame, m, HALO + r, 1) for m in range(members)], axis=1)
-        got = jnp.dot(pick, around, preferred_element_type=F32).astype(BF16)
-        for m in range(members):
-            part = got[:, m * wide : (m + 1) * wide]
-            at = pl.ds((m * rows + r) * obs_cols, obs_cols)
-            patch[at, pl.ds(0, wide)] = part[:obs_cols]
-            patch[at, pl.ds(wide, wide)] = part[obs_cols:]
-
-    for r in range(1, rows - 1):
-        observe(r)
-    for m in range(members):
-        pl.when(has_prev)(lambda: edge_next[m].wait_recv())
-        pl.when(has_next)(lambda: edge_prev[m].wait_recv())
-
-    @pl.when(tile == 0)
-    def _():
-        edge[0] = jnp.zeros(edge.shape[1:], BF16)
-
-    @pl.when(tile == tile_n - 1)
-    def _():
-        edge[1] = jnp.zeros(edge.shape[1:], BF16)
-
-    for m in range(members):
-        frame[m, HALO - 1] = with_sides(edge[0, m].astype(F32))
-        frame[m, HALO + rows] = with_sides(edge[1, m].astype(F32))
-    for r in sorted({0, rows - 1}):
-        observe(r)
-    spread_pred = lax.dot_general(
-        patch[...], big_obs[...], (((1,), (1,)), ((), ())), preferred_element_type=F32
-    )
-    spread_pred = spread_pred.reshape(members * rows, obs_cols, obs_lanes)
     first_lane = iota((1, obs_cols, obs_lanes), 1) * obs_ch
     lane = iota((1, obs_cols, obs_lanes), 2)
     own = (lane >= first_lane) & (lane < first_lane + obs_ch)
     per = members * rows
+
+    def observe(base, chosen):
+        for i, r in enumerate(chosen):
+            here = cells_t[:, r : r + 1]
+            pick = jnp.concatenate([(here == column), (here == column + 1)], axis=0).astype(BF16)
+            around = jnp.concatenate([taps(frame, m, HALO + r, 1) for m in range(members)], axis=1)
+            got = jnp.dot(pick, around, preferred_element_type=F32).astype(BF16)
+            for m in range(members):
+                part = got[:, m * wide : (m + 1) * wide]
+                at = pl.ds((base + i * members + m) * obs_cols, obs_cols)
+                patch[at, pl.ds(0, wide)] = part[:obs_cols]
+                patch[at, pl.ds(wide, wide)] = part[obs_cols:]
+        count = len(chosen) * members
+        spread_pred = lax.dot_general(
+            patch[pl.ds(base * obs_cols, count * obs_cols), :], big_obs[...], (((1,), (1,)), ((), ())),
+            preferred_element_type=F32,
+        ).reshape(count, obs_cols, obs_lanes)
+        found = jnp.sum(jnp.where(own, spread_pred, 0.0), axis=1)
+        for i, r in enumerate(chosen):
+            for m in range(members):
+                preds[pl.ds(me * per + m * rows + r, 1), :] = found[i * members + m : i * members + m + 1]
+
+    inner, outer = list(range(1, rows - 1)), sorted({0, rows - 1})
+    observe(0, inner)
+    for m in range(members):
+        pl.when(has_prev)(lambda: edge_next[m].wait_recv())
+        pl.when(has_next)(lambda: edge_prev[m].wait_recv())
+
+    @pl.when(tile == 0)
+    def _():
+        edge[0] = jnp.zeros(edge.shape[1:], BF16)
+
+    @pl.when(tile == tile_n - 1)
+    def _():
+        edge[1] = jnp.zeros(edge.shape[1:], BF16)
+
+    for m in range(members):
+        frame[m, HALO - 1] = with_sides(edge[0, m].astype(F32))
+        frame[m, HALO + rows] = with_sides(edge[1, m].astype(F32))
+    observe(len(inner) * members, outer)
     mine_at = pl.ds(pl.multiple_of(me * per, per), per)
-    preds[mine_at, :] = jnp.sum(jnp.where(own, spread_pred, 0.0), axis=1)
-
     pred_copies = [
         remote(preds.at[mine_at], preds.at[mine_at], pred_send.at[k], pred_recv.at[me], "mem", mem_peer(k))
         for k in range(1, mem_n)
@@ -349,8 +353,6 @@
         copy.start()
     for m in range(early, members):
         share(m)
-    for m in range(early):
-        pass_on(m)
     for k in range(1, mem_n):
         j = mem_peer(k)
         block = preds.at[pl.ds(pl.multiple_of(j * per, per), per)]
@@ -378,7 +380,7 @@
     for copy in cov_copies:
         copy.start()
 
-    for m in range(early, members):
+    for m in range(members):
         pass_on(m)
     for k in range(1, tile_n):
         j = tile_peer(k)
@@ -398,21 +400,21 @@
     for k in range(1, mem_n, step):
         for m in range(members):
             arrived(k, m)
-    def update_row(r, carry):
+    for r in range(rows):
         acc = [gathered[me, q, r].astype(F32) for q in range(members)]
         for j in range(ens):
             value = gathered[j // members, j % members, r].astype(F32)
             for q in range(members):
                 acc[q] = acc[q] + factors[q][j : j + 1] * value
         for q in range(members):
-            out[q, r] = acc[q]
-        return carry
-
-    lax.fori_loop(0, rows, update_row, 0)
-
-    pl.when(has_next)(lambda: to_next.wait_send())
-    pl.when(has_prev)(lambda: to_prev.wait_send())
-    for m in range(members):
+            stage[q, pl.ds(r, pairs, stride=rows), :] = acc[q]
+    for q in range(members):
+        for p in range(pairs):
+            out[q, :, pl.ds(p * lanes, lanes)] = stage[q, pl.ds(p * rows, rows), :]
+
+    for m in range(members):
+        pl.when(has_next)(lambda: to_next[m].wait_send())
+        pl.when(has_prev)(lambda: to_prev[m].wait_send())
         pl.when(has_next)(lambda: edge_next[m].wait_send())
         pl.when(has_prev)(lambda: edge_prev[m].wait_send())
     for copy in bulk + pred_copies + cov_copies + forwards:
@@ -437,7 +439,7 @@
     analysis, covariance = pl.pallas_call(
         functools.partial(kernel, sizes),
         out_shape=(
-            jax.ShapeDtypeStruct((members, rows, pairs, lanes), F32),
+            jax.ShapeDtypeStruct((members, rows, flat_count), F32),
             jax.ShapeDtypeStruct((ens, ens), F32),
         ),
         in_specs=[pl.BlockSpec(memory_space=pltpu.HBM)] * 7,
@@ -445,7 +447,7 @@
         scratch_shapes=[pltpu.VMEM(x.shape, x.dtype) for x in operands] + [
             dma((7,)),
             pltpu.VMEM((2, members, rows, flat_count), BF16),
-            pltpu.VMEM((pairs * rows, lanes), F32),
+            pltpu.VMEM((members, pairs * rows, lanes), F32),
             pltpu.VMEM((members, ext, pairs, lanes), BF16),
             pltpu.VMEM((members, ext, pairs, 2 * lanes), BF16),
             pltpu.VMEM((members, ext, pairs, 2 * hidden), BF16),
@@ -459,7 +461,7 @@
             pltpu.VMEM((mem_n * members * rows, obs_lanes), F32),
             pltpu.VMEM((obs_lanes // 128, ens * rows, 128), F32),
             pltpu.VMEM((tile_n, ens, 128), F32),
-            dma((2,)), dma((2,)), dma((2, members)), dma((2, members)),
+            dma((2, members)), dma((2, members)), dma((2, members)), dma((2, members)),
             dma((mem_n,)), dma((mem_n,)),
             dma((mem_n, members)), dma((mem_n, members)), dma((mem_n, members)),
             dma((tile_n,)), dma((tile_n,)),
@@ -468,7 +470,7 @@
             collective_id=0, has_side_effects=True, vmem_limit_bytes=56 * 1024 * 1024
         ),
     )(*operands)
-    return analysis.reshape(members, rows, flat_count), covariance
+    return analysis, covariance
 
 
 def solution(mesh):

time: 30.9 us -> 30.1 us (0.974)
  Pallas kernels: 27.8 us -> 27 us
    reshape x1 -> x0, local copies, waits for them, and re-layouts: 1.76 us -> none  [per_device(): return (analysis.reshape(members, rows, flat_count), covariance)]
    unnamed x3 -> x4, local copies, waits for them, and re-layouts: 0.6 us -> 2.28 us
    pallas_call x1, Pallas kernels: 27.8 us -> 27 us  [per_device(): pl.pallas_call(functools.partial(kernel, sizes), out_shape=(jax.ShapeDtyp...]
where the time goes in v3:
time: 30.1 us; the launch traced here: 29.9 us
  Pallas kernels  27 us (90%)
  local copies, waits for them, and re-layouts  2.28 us (8%)
  between operations  0.65 us (2%)
    pallas_call x1, Pallas kernels, per_device(): pl.pallas_call(functools.partial(kernel, sizes), out_shape=(jax.ShapeDtyp...  27 us
    unnamed x4, local copies, waits for them, and re-layouts  2.28 us

profile of v3, /device:TPU:0, one launch (start us, length us, event | category | flops | bytes accessed | tf_op | source)
XLA Modules:
  0.0 29.9 jit_solution(285723190009509863)
XLA Ops:
  0.6 27.0 %shard_map.86 = (f32[2,4,8192]{2,1,0:T(4,128)}, f32[16,16]{1,0:T(8,128)}) custom-call(bf16[2,4,8192]{2,1,0:T(4,128)(2,1)} %refs_0_.1, bf16[2,576,256]{2,1,0:T(8,128)(2,1)} %refs_1_.1, bf16[2,64,2304]{2,1,0:T(8,128)(2,1)} %bitcast.2, bf16[8,576]{1,0:T(8,128)(2,1)} %bitcast.3, s32[4,32]{1,0:T(4,128)} %refs_4_.1, f32[4,256]{1,0:T(4,128)} %refs_5_.1, ...), custom_call_target="tpu_custom_call" | custom-call | tf_op jit(solution)/shard_map/pallas_call | solution.py:439
  27.6 0.0 copy-start
  27.6 1.7 %copy.11 = f32[2,4,8192]{2,1,0:T(4,128)} copy(f32[2,4,8192]{2,1,0:T(4,128)} %get-tuple-element.4) | data formatting | bytes 524288
  29.3 0.0 copy-done
  29.3 0.6 %copy.12 = f32[16,16]{1,0:T(8,128)} copy(f32[16,16]{1,0:T(8,128)S(1)} %copy-done) | data formatting | bytes 2048
Async XLA Ops:
  27.6 1.7 %copy-start = (f32[16,16]{1,0:T(8,128)S(1)}, f32[16,16]{1,0:T(8,128)}, u32[]{:S(2)}) copy-start(f32[16,16]{1,0:T(8,128)} %get-tuple-element.5) | copy-start | bytes 3076

commit v4 on v3

--- a/solution.py
+++ b/solution.py
@@ -38,12 +38,12 @@
     sizes, *refs
 ):
     mem_n, tile_n = sizes
-    operands, (out, cov_out), local, load_sem, rest = refs[:7], refs[7:9], refs[9:16], refs[16], refs[17:]
+    operands, (gathered, cov_out), local, load_sem, rest = refs[:7], refs[7:9], refs[9:16], refs[16], refs[17:]
     lat, w_in, w_out, w_obs, cells, values, precision = local
     (
-    halo, stage, raw, frame, hid, cur, big_in, big_out, big_obs, patch, gathered, edge, preds, chunks, covs,
+    halo, stage, raw, frame, hid, cur, big_in, big_out, big_obs, patch, denoised, edge, preds, chunks, covs,
     halo_send, halo_recv, edge_send, edge_recv, pred_send, pred_recv,
-    bulk_send, fwd_send, bulk_recv, cov_send, cov_recv,
+    bulk_send, fwd_send, bulk_recv, cov_send, cov_recv, keep_sem,
     ) = rest
     members, rows, flat_count = lat.shape
     half = w_obs.shape[1] // 9
@@ -244,11 +244,11 @@
     edge_next, edge_prev, bulk, forwards = [], [], [], []
 
     def share(m):
-        block = gathered.at[me, m]
+        block, place = denoised.at[m], gathered.at[me, m]
         for k in range(step, mem_n, step):
-            bulk.append(remote(block, block, bulk_send.at[k, m], bulk_recv.at[me, m], "mem", mem_peer(k)))
+            bulk.append(remote(block, place, bulk_send.at[k, m], bulk_recv.at[me, m], "mem", mem_peer(k)))
         if step == 2:
-            bulk.append(remote(block, block, bulk_send.at[0, m], bulk_recv.at[me, m], "mem", sibling))
+            bulk.append(remote(block, place, bulk_send.at[0, m], bulk_recv.at[me, m], "mem", sibling))
         for copy in bulk[-(mem_n // step if step == 2 else mem_n - 1):]:
             copy.start()
 
@@ -277,18 +277,18 @@
         at = 0
         for m, r, count in picked:
             end = at + count * pairs
-            gathered[me, m, pl.ds(r, count)] = done[at:end].reshape(count, pairs, lanes)
+            denoised[m, pl.ds(r, count)] = done[at:end].reshape(count, pairs, lanes)
             put(frame, m, HALO + r, count, sides[at:end])
             at = end
 
     finish([(m, r, 1) for m in range(members) for r in sorted({0, rows - 1})])
     for m in range(members):
         edge_next.append(remote(
-            gathered.at[me, m, rows - 1], edge.at[0, m], edge_send.at[0, m], edge_recv.at[0, m],
+            denoised.at[m, rows - 1], edge.at[0, m], edge_send.at[0, m], edge_recv.at[0, m],
             "tile", jnp.minimum(tile + 1, tile_n - 1),
         ))
         edge_prev.append(remote(
-            gathered.at[me, m, 0], edge.at[1, m], edge_send.at[1, m], edge_recv.at[1, m],
+            denoised.at[m, 0], edge.at[1, m], edge_send.at[1, m], edge_recv.at[1, m],
             "tile", jnp.maximum(tile - 1, 0),
         ))
         pl.when(has_next)(lambda: edge_next[m].start())
@@ -296,6 +296,8 @@
     finish([(m, 1, rows - 2) for m in range(members)])
     for m in range(early):
         share(m)
+    keep = pltpu.make_async_copy(denoised, gathered.at[me], keep_sem)
+    keep.start()
 
     column = 2 * iota((obs_cols, pairs), 1)
     wide = 12 * half
@@ -390,16 +392,31 @@
         cov = cov + covs[j]
     cov = cov[:, :ens] * (1.0 / (rows * tile_n * obs_lanes))
     cov_out[...] = cov
+    for k in range(1, mem_n, step):
+        for m in range(members):
+            arrived(k, m)
+    keep.wait()
+    for m in range(members):
+        pl.when(has_next)(lambda: to_next[m].wait_send())
+        pl.when(has_prev)(lambda: to_prev[m].wait_send())
+        pl.when(has_next)(lambda: edge_next[m].wait_send())
+        pl.when(has_prev)(lambda: edge_prev[m].wait_send())
+    for copy in bulk + pred_copies + cov_copies + forwards:
+        copy.wait_send()
+
+
+def update_kernel(gathered, cov_ref, out, cov_out, stage):
+    mem_n, members, rows, pairs, lanes = gathered.shape
+    ens = mem_n * members
+    me = lax.axis_index("mem")
+    cov = cov_ref[...]
+    cov_out[...] = cov
     centred = GUIDE_STEP * (cov - jnp.mean(cov, axis=0, keepdims=True))
     factors = []
     for q in range(members):
         mine = iota((ens, ens), 1) == me * members + q
         column_q = jnp.sum(jnp.where(mine, centred, 0.0), axis=1, keepdims=True)
         factors.append(jnp.broadcast_to(column_q, (ens, lanes)))
-
-    for k in range(1, mem_n, step):
-        for m in range(members):
-            arrived(k, m)
     for r in range(rows):
         acc = [gathered[me, q, r].astype(F32) for q in range(members)]
         for j in range(ens):
@@ -411,14 +428,6 @@
     for q in range(members):
         for p in range(pairs):
             out[q, :, pl.ds(p * lanes, lanes)] = stage[q, pl.ds(p * rows, rows), :]
-
-    for m in range(members):
-        pl.when(has_next)(lambda: to_next[m].wait_send())
-        pl.when(has_prev)(lambda: to_prev[m].wait_send())
-        pl.when(has_next)(lambda: edge_next[m].wait_send())
-        pl.when(has_prev)(lambda: edge_prev[m].wait_send())
-    for copy in bulk + pred_copies + cov_copies + forwards:
-        copy.wait_send()
 
 
 def per_device(sizes, latents, in_weight, out_weight, observe_weight, obs_cells, obs_values, obs_precision):
@@ -436,14 +445,14 @@
     )
     vmem = pl.BlockSpec(memory_space=pltpu.VMEM)
     dma = pltpu.SemaphoreType.DMA
-    analysis, covariance = pl.pallas_call(
+    everyone, covariance = pl.pallas_call(
         functools.partial(kernel, sizes),
         out_shape=(
-            jax.ShapeDtypeStruct((members, rows, flat_count), F32),
+            jax.ShapeDtypeStruct((mem_n, members, rows, pairs, lanes), BF16),
             jax.ShapeDtypeStruct((ens, ens), F32),
         ),
         in_specs=[pl.BlockSpec(memory_space=pltpu.HBM)] * 7,
-        out_specs=(vmem, vmem),
+        out_specs=(pl.BlockSpec(memory_space=pltpu.HBM), vmem),
         scratch_shapes=[pltpu.VMEM(x.shape, x.dtype) for x in operands] + [
             dma((7,)),
             pltpu.VMEM((2, members, rows, flat_count), BF16),
@@ -456,7 +465,7 @@
             pltpu.VMEM((2, 2 * lanes, 6 * hidden), BF16),
             pltpu.VMEM((obs_lanes, 24 * half), BF16),
             pltpu.VMEM((members * rows * obs_cols, 24 * half), BF16),
-            pltpu.VMEM((mem_n, members, rows, pairs, lanes), BF16),
+            pltpu.VMEM((members, rows, pairs, lanes), BF16),
             pltpu.VMEM((2, members, pairs, lanes), BF16),
             pltpu.VMEM((mem_n * members * rows, obs_lanes), F32),
             pltpu.VMEM((obs_lanes // 128, ens * rows, 128), F32),
@@ -464,13 +473,27 @@
             dma((2, members)), dma((2, members)), dma((2, members)), dma((2, members)),
             dma((mem_n,)), dma((mem_n,)),
             dma((mem_n, members)), dma((mem_n, members)), dma((mem_n, members)),
-            dma((tile_n,)), dma((tile_n,)),
+            dma((tile_n,)), dma((tile_n,)), dma,
         ],
         compiler_params=pltpu.CompilerParams(
             collective_id=0, has_side_effects=True, vmem_limit_bytes=56 * 1024 * 1024
         ),
     )(*operands)
-    return analysis, covariance
+    count = 2 if pairs % 32 == 0 else 1
+    part = pairs // count
+    whole = pl.BlockSpec((ens, ens), lambda i: (0, 0))
+    return pl.pallas_call(
+        update_kernel,
+        grid=(count,),
+        out_shape=(
+            jax.ShapeDtypeStruct((members, rows, flat_count), F32),
+            jax.ShapeDtypeStruct((ens, ens), F32),
+        ),
+        in_specs=[pl.BlockSpec((mem_n, members, rows, part, lanes), lambda i: (0, 0, 0, i, 0)), whole],
+        out_specs=(pl.BlockSpec((members, rows, part * lanes), lambda i: (0, 0, i)), whole),
+        scratch_shapes=[pltpu.VMEM((members, part * rows, lanes), F32)],
+        compiler_params=pltpu.CompilerParams(vmem_limit_bytes=56 * 1024 * 1024),
+    )(everyone, covariance)
 
 
 def solution(mesh):

time: 30.1 us -> 29.6 us (0.983)
  local copies, waits for them, and re-layouts: 2.28 us -> 0 us
  Pallas kernels: 27 us -> 28.8 us
    pallas_call x0 -> x1, Pallas kernels: none -> 2.34 us  [per_device(): pl.pallas_call(update_kernel, grid=(count,), out_shape=(jax.ShapeDtypeStr...]
    unnamed x4 -> x0, local copies, waits for them, and re-layouts: 2.28 us -> none
    pallas_call x1, Pallas kernels: 27 us -> 26.4 us  [per_device(): pl.pallas_call(functools.partial(kernel, sizes), out_shape=(jax.ShapeDtyp...]
where the time goes in v4:
time: 29.6 us; the launch traced here: 29.4 us
  Pallas kernels  28.8 us (97%)
  between operations  0.64 us (2%)
    pallas_call x1, Pallas kernels, per_device(): pl.pallas_call(functools.partial(kernel, sizes), out_shape=(jax.ShapeDtyp...  26.4 us
    pallas_call x1, Pallas kernels, per_device(): pl.pallas_call(update_kernel, grid=(count,), out_shape=(jax.ShapeDtypeStr...  2.34 us

profile of v4, /device:TPU:0, one launch (start us, length us, event | category | flops | bytes accessed | tf_op | source)
XLA Modules:
  0.0 29.4 jit_solution(3055920653068462278)
XLA Ops:
  0.6 26.4 %shard_map.86 = (bf16[8,2,4,64,128]{4,3,2,1,0:T(8,128)(2,1)}, f32[16,16]{1,0:T(8,128)}) custom-call(bf16[2,4,8192]{2,1,0:T(4,128)(2,1)} %refs_0_.1, bf16[2,576,256]{2,1,0:T(8,128)(2,1)} %refs_1_.1, bf16[2,64,2304]{2,1,0:T(8,128)(2,1)} %bitcast.2, bf16[8,576]{1,0:T(8,128)(2,1)} %bitcast.3, s32[4,32]{1,0:T(4,128)} %refs_4_.1, f32[4,256]{1,0:T(4,128)} %refs_5_.1, ...), custom_call_target="tpu_custom_call" | custom-call | tf_op jit(solution)/shard_map/pallas_call | solution.py:448
  27.1 2.3 %shard_map.87 = (f32[2,4,8192]{2,1,0:T(4,128)}, f32[16,16]{1,0:T(8,128)}) custom-call(bf16[8,2,4,64,128]{4,3,2,1,0:T(8,128)(2,1)} %get-tuple-element.4.gathered, f32[16,16]{1,0:T(8,128)} %get-tuple-element.5.cov_ref), custom_call_target="tpu_custom_call" | custom-call | tf_op jit(solution)/shard_map/pallas_call | solution.py:485

commit v5 on v4

--- a/solution.py
+++ b/solution.py
@@ -41,7 +41,7 @@
     operands, (gathered, cov_out), local, load_sem, rest = refs[:7], refs[7:9], refs[9:16], refs[16], refs[17:]
     lat, w_in, w_out, w_obs, cells, values, precision = local
     (
-    halo, stage, raw, frame, hid, cur, big_in, big_out, big_obs, patch, denoised, edge, preds, chunks, covs,
+    halo, stage, raw, frame, hid, cur, big_in, big_out, turned, big_obs, patch, denoised, edge, preds, chunks, covs,
     halo_send, halo_recv, edge_send, edge_recv, pred_send, pred_recv,
     bulk_send, fwd_send, bulk_recv, cov_send, cov_recv, keep_sem,
     ) = rest
@@ -109,6 +109,8 @@
                 at = pl.ds(b * half, half)
                 big_out[layer, at, pl.ds(di * 2 * hidden, hidden)] = even
                 big_out[layer, at, pl.ds((di * 2 + 1) * hidden, hidden)] = odd
+            at = pl.ds(di * 2 * hidden, 2 * hidden)
+            turned[layer, at, :] = big_out[layer, :, at].T
 
     def build_obs():
         weight = w_obs[...]
@@ -122,7 +124,7 @@
         spread_ch = jnp.concatenate([same_ch] * obs_cols, axis=0)
         big_obs[...] = jnp.dot(
             spread_ch.astype(BF16), jnp.concatenate(blocks, axis=1), preferred_element_type=F32
-        ).astype(BF16)
+        ).astype(BF16).T
 
     def unfold(slot, source, m):
         for p in range(pairs):
@@ -170,9 +172,7 @@
         put(hid, m, start, count, act.astype(BF16))
 
     def conv_sum(layer, lhs, before):
-        summed = lax.dot_general(
-            lhs, big_out[layer], (((1,), (1,)), ((), ())), preferred_element_type=F32
-        )
+        summed = jnp.dot(lhs, turned[layer], preferred_element_type=F32)
         summed = summed[:, :lanes] + neighbours(summed[:, lanes:], pairs, half, True)
         return (before.astype(F32) + summed).astype(BF16)
 
@@ -319,9 +319,8 @@
                 patch[at, pl.ds(0, wide)] = part[:obs_cols]
                 patch[at, pl.ds(wide, wide)] = part[obs_cols:]
         count = len(chosen) * members
-        spread_pred = lax.dot_general(
-            patch[pl.ds(base * obs_cols, count * obs_cols), :], big_obs[...], (((1,), (1,)), ((), ())),
-            preferred_element_type=F32,
+        spread_pred = jnp.dot(
+            patch[pl.ds(base * obs_cols, count * obs_cols), :], big_obs[...], preferred_element_type=F32
         ).reshape(count, obs_cols, obs_lanes)
         found = jnp.sum(jnp.where(own, spread_pred, 0.0), axis=1)
         for i, r in enumerate(chosen):
@@ -463,7 +462,8 @@
             pltpu.VMEM((members, ext, pairs, lanes), BF16),
             pltpu.VMEM((2, 12 * half, 2 * hidden), BF16),
             pltpu.VMEM((2, 2 * lanes, 6 * hidden), BF16),
-            pltpu.VMEM((obs_lanes, 24 * half), BF16),
+            pltpu.VMEM((2, 6 * hidden, 2 * lanes), BF16),
+            pltpu.VMEM((24 * half, obs_lanes), BF16),
             pltpu.VMEM((members * rows * obs_cols, 24 * half), BF16),
             pltpu.VMEM((members, rows, pairs, lanes), BF16),
             pltpu.VMEM((2, members, pairs, lanes), BF16),

time: 29.6 us -> 29.3 us (0.990)
  Pallas kernels: 28.8 us -> 28.5 us
where the time goes in v5:
time: 29.3 us; the launch traced here: 29.2 us
  Pallas kernels  28.5 us (97%)
  between operations  0.64 us (2%)
    pallas_call x1, Pallas kernels, per_device(): pl.pallas_call(functools.partial(kernel, sizes), out_shape=(jax.ShapeDtyp...  26.2 us
    pallas_call x1, Pallas kernels, per_device(): pl.pallas_call(update_kernel, grid=(count,), out_shape=(jax.ShapeDtypeStr...  2.34 us

profile of v5, /device:TPU:0, one launch (start us, length us, event | category | flops | bytes accessed | tf_op | source)
XLA Modules:
  0.0 29.2 jit_solution(670266831973730550)
XLA Ops:
  0.6 26.2 %shard_map.86 = (bf16[8,2,4,64,128]{4,3,2,1,0:T(8,128)(2,1)}, f32[16,16]{1,0:T(8,128)}) custom-call(bf16[2,4,8192]{2,1,0:T(4,128)(2,1)} %refs_0_.1, bf16[2,576,256]{2,1,0:T(8,128)(2,1)} %refs_1_.1, bf16[2,64,2304]{2,1,0:T(8,128)(2,1)} %bitcast.2, bf16[8,576]{1,0:T(8,128)(2,1)} %bitcast.3, s32[4,32]{1,0:T(4,128)} %refs_4_.1, f32[4,256]{1,0:T(4,128)} %refs_5_.1, ...), custom_call_target="tpu_custom_call" | custom-call | tf_op jit(solution)/shard_map/pallas_call | solution.py:447
  26.8 2.3 %shard_map.87 = (f32[2,4,8192]{2,1,0:T(4,128)}, f32[16,16]{1,0:T(8,128)}) custom-call(bf16[8,2,4,64,128]{4,3,2,1,0:T(8,128)(2,1)} %get-tuple-element.4.gathered, f32[16,16]{1,0:T(8,128)} %get-tuple-element.5.cov_ref), custom_call_target="tpu_custom_call" | custom-call | tf_op jit(solution)/shard_map/pallas_call | solution.py:485
